TPU v7x, 32 devices: a whole 2x2x4 slice. The times are simulated.
32 devices in a mesh: groups: 2 (over y), band: 4 (over z), sector: 2 (over x), chan: 2 (over core).
Axes of the slice: x: 2, y: 2, z: 4, core: 2. Of those that a mesh axis runs over, the one named last changes fastest.
Arguments:
- grid_inputs: bfloat16 [8, 2, 2048, 227], P(('groups', 'band'), 'sector'), parts along dimension 0, may hold values from -6 to 6
- mesh_node_embedding: bfloat16 [8, 2, 256, 512], P(('groups', 'band'), 'sector', None, 'chan'), parts along dimension 0, may hold values from -6 to 6
- enc_counts: int32 [4, 2, 4], P('band', 'sector'), may hold values from 1 to 4, as said below
- enc_source: int32 [4, 2, 8], P('band', 'sector'), may hold values from 0 to 15
- enc_target: int32 [4, 2, 8], P('band', 'sector'), may hold values from 0 to 1
- enc_blocks: bfloat16 [4, 2, 8, 128, 128], P('band', 'sector'), may hold values from -0.25 to 0.25
- proc_source: int32 [4, 2, 8], P('band', 'sector'), may hold values from 0 to 3, as said below
- proc_target: int32 [4, 2, 8], P('band', 'sector'), may hold values from 0 to 1
- proc_blocks: bfloat16 [4, 2, 8, 128, 128], P('band', 'sector'), may hold values from -0.25 to 0.25
- bound_blocks: int32 [4, 2, 2, 1], P('band', 'sector'), may hold values from 0 to 1
- dec_blocks: bfloat16 [4, 2, 8, 128, 128], P('band', 'sector'), may hold values from -0.5 to 0.5
- grid_w1: bfloat16 [227, 512], P(None, 'chan'), may hold values from -0.375 to 0.375
- grid_gain: float32 [512], replicated, may hold values from 0.1 to 1.9
- grid_w2: bfloat16 [512, 512], P(None, 'chan'), may hold values from -0.25 to 0.25
- enc_w1: bfloat16 [2, 512, 512], P(None, None, 'chan'), may hold values from -0.1875 to 0.1875
- enc_gain: float32 [512], replicated, may hold values from 0.1 to 1.9
- enc_w2: bfloat16 [512, 512], P(None, 'chan'), may hold values from -0.25 to 0.25
- proc_w1: bfloat16 [2, 512, 512], P(None, None, 'chan'), may hold values from -0.1875 to 0.1875
- proc_gain: float32 [512], replicated, may hold values from 0.1 to 1.9
- processor_second_weight: bfloat16 [512, 512], P(None, 'chan'), may hold values from -0.25 to 0.25
- dec_w1: bfloat16 [2, 512, 512], P(None, None, 'chan'), may hold values from -0.1875 to 0.1875
- dec_gain: float32 [512], replicated, may hold values from 0.1 to 1.9
- dec_w2: bfloat16 [512, 227], replicated, may hold values from -0.25 to 0.25
Outputs:
- prediction: float32 [8, 2, 2048, 227], P(('groups', 'band'), 'sector'), parts along dimension 0
There are 2 independent parts, one for each index of `groups`. A program takes and returns all parts, laid end to end along the dimension named above; an argument that names none is the same for every part. Nothing has to cross between parts.
Inputs may be any that keep to these rules, and one draw needn't show every extreme that they name: `enc_counts`: for each band and sector, its 8 encoder edge blocks are ordered by receiving band; each band receives 1 to 4 of them, they sum to 8, and in each sector one band receives exactly 4 from every band. `proc_source`: values below 2 are own blocks, then 1 from the previous sector, then 1 from the next; edge block k < 2 reads source 2 + k.
All inputs are finite; a program needn't handle non-finite values.
Results may differ from a plain program's by a relative error of at most 0.011.
Values may be sent and summed in bfloat16 or wider, within the bound.
A program may use at most 64 MiB of HBM per device.

v0:
```python
import jax
import jax.numpy as jnp
from jax import lax
from jax.sharding import PartitionSpec as P

G_BLK = 16
M_BLK = 2
CAP = 4
BND = 1


def as_sent(shard):

    def short(part):
        return part.astype(jnp.bfloat16) if part.dtype == jnp.float32 else part

    return jax.tree.map(short, shard)


def extended_2(shard, sides, width):
    for axis, dim in sides:
        devices, length = (lax.axis_size(axis), shard.shape[dim])
        up = [(i, (i + 1) % devices) for i in range(devices)]
        down = [(j, i) for i, j in up]
        last = lax.slice_in_dim(shard, length - width, length, axis=dim)
        first = lax.slice_in_dim(shard, 0, width, axis=dim)
        before = lax.ppermute(last, axis, up)
        after = lax.ppermute(first, axis, down)
        shard = jnp.concatenate([before, shard, after], axis=dim)
    return shard


def matmul(left, right):
    return jnp.dot(left, right, preferred_element_type=jnp.float32)


def norm_silu(pre_act, gain):
    values = pre_act.astype(jnp.float32)
    center = values - jnp.mean(values, axis=-1, keepdims=True)
    spread = jnp.mean(center * center, axis=-1, keepdims=True)
    return jax.nn.silu(center * lax.rsqrt(spread + 1e-05) * gain).astype(jnp.bfloat16)


def widen(block_pieces):
    return jax.tree.map(
        lambda part, own: part.astype(own.dtype),
        lax.all_gather(as_sent(block_pieces), "chan", axis=1, tiled=True),
        block_pieces,
    )


def hidden_map(pre_act, gain, w_out):
    full_pre = widen(pre_act.astype(jnp.bfloat16))
    return matmul(norm_silu(full_pre, gain), w_out)


def mesh_update(state, summed, w_in, gain, w_out):
    full_state, full_sum = widen((state, summed))
    pre_act = matmul(full_state, w_in[0]) + matmul(full_sum, w_in[1])
    return (state.astype(jnp.float32) + hidden_map(pre_act, gain, w_out)).astype(jnp.bfloat16)


def block_products(blocks, rows):
    return jnp.einsum("eij,ejf->eif", blocks, rows, preferred_element_type=jnp.float32).astype(
        jnp.bfloat16
    )


def local(
    grid_inputs,
    mesh_node_embedding,
    enc_counts,
    enc_source,
    enc_target,
    enc_blocks,
    proc_source,
    proc_target,
    proc_blocks,
    bound_blocks,
    dec_blocks,
    grid_w1,
    grid_gain,
    grid_w2,
    enc_w1,
    enc_gain,
    enc_w2,
    proc_w1,
    proc_gain,
    processor_second_weight,
    dec_w1,
    dec_gain,
    dec_w2,
):
    block_rows = enc_blocks.shape[-1]
    edge_count = enc_blocks.shape[2]
    band_count = enc_counts.shape[-1]
    grid_latent = hidden_map(matmul(grid_inputs[0, 0], grid_w1), grid_gain, grid_w2).astype(
        jnp.bfloat16
    )
    local_width = grid_latent.shape[1]
    grid_blocks = grid_latent.reshape(G_BLK, block_rows, local_width)
    sources = enc_source[0, 0]
    targets = enc_target[0, 0]
    enc_message = block_products(enc_blocks[0, 0], jnp.take(grid_blocks, sources, axis=0))
    peer_counts = enc_counts[0, 0]
    count_ends = jnp.cumsum(peer_counts)
    edge_ids = jnp.arange(edge_count, dtype=jnp.int32)
    peer_of = jnp.sum((count_ends[None, :] <= edge_ids[:, None]).astype(jnp.int32), axis=1)
    slot_of = edge_ids - jnp.take(count_ends - peer_counts, peer_of)
    slot_index = peer_of * CAP + slot_of
    placement = (
        jnp.arange(band_count * CAP, dtype=jnp.int32)[:, None] == slot_index[None, :]
    ).astype(jnp.bfloat16)
    target_hot = (targets[:, None] == jnp.arange(M_BLK, dtype=jnp.int32)[None, :]).astype(
        jnp.bfloat16
    )
    send_hot = matmul(placement, target_hot).astype(jnp.bfloat16).reshape(band_count, CAP, M_BLK)
    send_rows = jnp.einsum(
        "se,erf->srf", placement, enc_message, preferred_element_type=jnp.float32
    ).astype(jnp.bfloat16)
    send_rows = send_rows.reshape(band_count, CAP, block_rows, local_width)
    recv_rows, receiver_onehot = (
        lax.all_to_all(send_rows, "band", split_axis=0, concat_axis=0, tiled=True),
        lax.all_to_all(send_hot, "band", split_axis=0, concat_axis=0, tiled=True),
    )
    enc_part = jnp.einsum(
        "pcd,pcrf->pdrf", receiver_onehot, recv_rows, preferred_element_type=jnp.float32
    ).astype(jnp.bfloat16)
    enc_sum = jnp.sum(enc_part.astype(jnp.float32), axis=0)
    enc_sum = enc_sum.astype(jnp.bfloat16).reshape(M_BLK * block_rows, local_width)
    mesh_one = mesh_update(mesh_node_embedding[0, 0], enc_sum, enc_w1, enc_gain, enc_w2)
    mesh_blocks = mesh_one.reshape(M_BLK, block_rows, local_width)
    listed = jnp.take(mesh_blocks, bound_blocks[0, 0].reshape(2 * BND), axis=0)
    extended = extended_2(listed, (("sector", 0),), BND)
    proc_sources = jnp.concatenate([mesh_blocks, extended[:BND], extended[-BND:]], axis=0)
    processor_edge_message = block_products(
        proc_blocks[0, 0], jnp.take(proc_sources, proc_source[0, 0], axis=0)
    )
    processor_onehot = (
        proc_target[0, 0][:, None] == jnp.arange(M_BLK, dtype=jnp.int32)[None, :]
    ).astype(jnp.bfloat16)
    processor_edge_sum = jnp.einsum(
        "qi,qkg->ikg", processor_onehot, processor_edge_message, preferred_element_type=jnp.float32
    )
    processor_edge_sum = processor_edge_sum.astype(jnp.bfloat16).reshape(
        M_BLK * block_rows, local_width
    )
    mesh_two = mesh_update(
        mesh_one, processor_edge_sum, proc_w1, proc_gain, processor_second_weight
    )
    coarse_mesh_blocks = mesh_two.reshape(M_BLK, block_rows, local_width)
    answer = jnp.einsum(
        "ksn,nbz->ksbz", receiver_onehot, coarse_mesh_blocks, preferred_element_type=jnp.float32
    ).astype(jnp.bfloat16)
    returned = lax.all_to_all(answer, "band", split_axis=0, concat_axis=0, tiled=True)
    returned = returned.reshape(band_count * CAP, block_rows, local_width)
    dec_rows = jnp.einsum(
        "se,srf->erf", placement, returned, preferred_element_type=jnp.float32
    ).astype(jnp.bfloat16)
    dec_message = block_products(dec_blocks[0, 0], dec_rows)
    grid_hot = (sources[:, None] == jnp.arange(G_BLK, dtype=jnp.int32)[None, :]).astype(
        jnp.bfloat16
    )
    dec_sum = jnp.einsum("eg,erf->grf", grid_hot, dec_message, preferred_element_type=jnp.float32)
    dec_sum = dec_sum.astype(jnp.bfloat16).reshape(G_BLK * block_rows, local_width)
    full_latent, full_sum = widen((grid_latent, dec_sum))
    dec_pre = matmul(full_latent, dec_w1[0]) + matmul(full_sum, dec_w1[1])
    prediction = hidden_map(dec_pre, dec_gain, dec_w2)
    return prediction[None, None]


def solution(mesh):
    in_specs = (
        P(("groups", "band"), "sector", None, None),
        P(("groups", "band"), "sector", None, "chan"),
        P("band", "sector", None),
        P("band", "sector", None),
        P("band", "sector", None),
        P("band", "sector", None, None, None),
        P("band", "sector", None),
        P("band", "sector", None),
        P("band", "sector", None, None, None),
        P("band", "sector", None, None),
        P("band", "sector", None, None, None),
        P(None, "chan"),
        P(),
        P(None, "chan"),
        P(None, None, "chan"),
        P(),
        P(None, "chan"),
        P(None, None, "chan"),
        P(),
        P(None, "chan"),
        P(None, None, "chan"),
        P(),
        P(),
    )
    out_specs = P(("groups", "band"), "sector", None, None)
    return jax.shard_map(local, mesh=mesh, in_specs=in_specs, out_specs=out_specs, check_vma=False)
```

profile of v0, /device:TPU:25, one launch (start us, length us, event | category | flops | bytes accessed | tf_op | source)
XLA Modules:
  0.0 157.7 jit_solution(17407510621989905924)
XLA Ops:
  6.6 1.1 copy-done
  7.7 2.4 %convolution_convert_fusion.1 = bf16[2048,256]{1,0:T(8,128)(2,1)} fusion(bf16[227,256]{1,0:T(8,128)(2,1)} %param.34, bf16[1,1,2048,227]{2,3,1,0:T(8,128)(2,1)S(1)} %copy-done), kind=kOutput, calls=%fused_computation.32 | convolution fusion | flops 238551040 | bytes 2094592 | tf_op jit(solution)/shard_map/dot_general | solution.py:34
  10.2 0.2 reduce-window.8
  10.4 0.6 gather_fusion
  11.1 0.3 convolution_convert_fusion.11
  11.4 0.6 copy.62
  12.0 4.5 %all-to-all-start = ((bf16[4,4,2]{1,2,0:T(2,128)(2,1)}), bf16[4,4,2]{1,2,0:T(2,128)(2,1)S(1)}, u32[]{:S(2)}, u32[]{:S(2)}) async-start(bf16[4,4,2]{1,2,0:T(2,128)(2,1)} %copy.62), calls=%async_computation | async-start | bytes 4096 | tf_op jit(solution)/shard_map/all_to_all | solution.py:124
  16.6 5.7 %all-gather.6.cloned.1.call-done = bf16[2048,512]{1,0:T(8,128)(2,1)} async-done(((bf16[2048,256]{1,0:T(8,128)(2,1)}), bf16[2048,512]{1,0:T(8,128)(2,1)}) %all-gather.6.cloned.1.call-update) | async-done | bytes 2097168 | tf_op jit(solution)/shard_map/all_gather | solution.py:47
  22.3 2.1 %convert_reduce_fusion.1 = f32[2048]{0:T(1024)S(1)} fusion(bf16[2048,512]{1,0:T(8,128)(2,1)} %all-gather.6.cloned.1.call-done), kind=kLoop, calls=%fused_computation.7 | loop fusion | flops 2095104 | bytes 2105344 | tf_op jit(solution)/shard_map/reduce_sum | solution.py:39
  24.4 0.1 copy-done.1
  24.6 1.0 fusion.12
  25.6 1.8 %convolution_convert_fusion = bf16[2048,256]{1,0:T(8,128)(2,1)S(1)} fusion(bf16[512,256]{1,0:T(8,128)(2,1)S(1)} %copy-done.12, bf16[2048,512]{1,0:T(8,128)(2,1)S(1)} %copy-done.1, f32[512]{0:T(512)S(1)} %copy-done.16, f32[2048]{0:T(1024)S(1)} %add_rsqrt_fusion.1, f32[2048]{0:T(1024)S(1)} %broadcast_multiply_fusion.1), kind=kOutput, calls=%fused_computation.31 | convolution fusion | flops 546832384 | bytes 3426304 | tf_op jit(solution)/shard_map/dot_general | solution.py:34
  27.5 0.6 gather_fusion.1
  28.1 0.4 fusion.26
  28.5 0.4 copy.64
  28.9 0.5 convolution_convert_fusion.4
  29.5 0.3 reshape.247
  29.8 1.3 copy.65
  31.2 4.7 %all-to-all-start.1 = ((bf16[4,4,128,256]{3,1,2,0:T(4,128)(2,1)}), bf16[4,4,128,256]{3,1,2,0:T(4,128)(2,1)S(1)}, u32[]{:S(2)}, u32[]{:S(2)}) async-start(bf16[4,4,128,256]{3,1,2,0:T(4,128)(2,1)} %copy.65), calls=%async_computation.1 | async-start | bytes 2097152 | tf_op jit(solution)/shard_map/all_to_all | solution.py:123
  35.8 2.4 %all-gather = bf16[1,1,256,512]{3,2,1,0:T(8,128)(2,1)S(1)} all-gather(bf16[1,1,256,256]{3,2,1,0:T(8,128)(2,1)S(1)} %copy-done.9), channel_id=2, replica_groups=mesh['groups'=2,'band'=4,'sector'=2,'chan'=2] {'chan'}, dimensions={3}, use_global_device_ids=true | all-gather | bytes 393216 | tf_op jit(solution)/shard_map/all_gather | solution.py:47
  38.3 0.2 fusion.71
  38.6 20.5 %all-to-all-done.1 = bf16[4,4,128,256]{3,1,2,0:T(4,128)(2,1)S(1)} async-done(((bf16[4,4,128,256]{3,1,2,0:T(4,128)(2,1)}), bf16[4,4,128,256]{3,1,2,0:T(4,128)(2,1)S(1)}, u32[]{:S(2)}, u32[]{:S(2)}) %all-to-all-start.1) | async-done | bytes 1048608 | tf_op jit(solution)/shard_map/all_to_all | solution.py:123
  59.1 0.8 fusion.29
  59.9 3.0 %all_gather.33 = bf16[256,512]{1,0:T(8,128)(2,1)S(1)} all-gather(bf16[256,256]{1,0:T(8,128)(2,1)S(1)} %bitcast.123), channel_id=1, replica_groups=mesh['groups'=2,'band'=4,'sector'=2,'chan'=2] {'chan'}, dimensions={1}, use_global_device_ids=true | all-gather | bytes 393216 | tf_op jit(solution)/shard_map/all_gather | solution.py:47
  62.9 0.2 fusion.30
  63.1 2.0 %all_gather.34 = bf16[256,512]{1,0:T(8,128)(2,1)S(1)} all-gather(bf16[256,256]{1,0:T(8,128)(2,1)S(1)} %fusion.30), channel_id=1, replica_groups=mesh['groups'=2,'band'=4,'sector'=2,'chan'=2] {'chan'}, dimensions={1}, use_global_device_ids=true | all-gather | bytes 393216 | tf_op jit(solution)/shard_map/all_gather | solution.py:47
  65.3 0.2 fusion.48
  65.5 0.4 fusion.31
  65.9 2.1 %all_gather.35 = bf16[256,512]{1,0:T(8,128)(2,1)S(1)} all-gather(bf16[256,256]{1,0:T(8,128)(2,1)S(1)} %fusion.31), channel_id=1, replica_groups=mesh['groups'=2,'band'=4,'sector'=2,'chan'=2] {'chan'}, dimensions={1}, use_global_device_ids=true | all-gather | bytes 393216 | tf_op jit(solution)/shard_map/all_gather | solution.py:47
  68.0 0.6 gather_fusion.2
  68.7 1.2 collective-permute-start.1
  69.9 0.3 collective-permute-start
  70.2 0.2 fusion.67
  70.5 1.4 collective-permute-done.1
  71.9 1.5 collective-permute-done
  73.5 0.6 gather_fusion.3
  74.1 0.4 fusion.27
  74.5 0.4 copy.68
  74.9 0.3 convolution_convert_fusion.10
  75.2 3.1 %all_gather.36 = bf16[256,512]{1,0:T(8,128)(2,1)S(1)} all-gather(bf16[256,256]{1,0:T(8,128)(2,1)S(1)} %bitcast.124), channel_id=1, replica_groups=mesh['groups'=2,'band'=4,'sector'=2,'chan'=2] {'chan'}, dimensions={1}, use_global_device_ids=true | all-gather | bytes 393216 | tf_op jit(solution)/shard_map/all_gather | solution.py:47
  78.3 0.2 fusion.32
  78.5 2.0 %all_gather.37 = bf16[256,512]{1,0:T(8,128)(2,1)S(1)} all-gather(bf16[256,256]{1,0:T(8,128)(2,1)S(1)} %fusion.32), channel_id=1, replica_groups=mesh['groups'=2,'band'=4,'sector'=2,'chan'=2] {'chan'}, dimensions={1}, use_global_device_ids=true | all-gather | bytes 393216 | tf_op jit(solution)/shard_map/all_gather | solution.py:47
  80.7 0.2 fusion.40
  80.9 0.4 fusion.33
  81.3 1.8 %convolution_convert_fusion.3 = bf16[4,4,128,256]{3,1,2,0:T(4,128)(2,1)} fusion(bf16[2,128,256]{2,1,0:T(8,128)(2,1)S(1)} %bitcast.125, bf16[4,4,2]{1,2,0:T(2,128)(2,1)S(1)} %all-to-all-done), kind=kOutput, calls=%fused_computation.37 | convolution fusion | flops 2621440 | bytes 1179712 | tf_op jit(solution)/shard_map/ksn,nbz->ksbz/dot_general | solution.py:152
  83.1 5.6 %all-to-all-start.2 = ((bf16[4,4,128,256]{3,1,2,0:T(4,128)(2,1)}), bf16[4,4,128,256]{3,1,2,0:T(4,128)(2,1)S(1)}, u32[]{:S(2)}, u32[]{:S(2)}) async-start(bf16[4,4,128,256]{3,1,2,0:T(4,128)(2,1)} %convolution_convert_fusion.3), calls=%async_computation.2 | async-start | bytes 2097152 | tf_op jit(solution)/shard_map/all_to_all | solution.py:155
  88.7 0.7 all-gather.8.cloned.1.call-update
  89.4 0.2 all-gather.10.cloned.1.call-start
  89.7 22.4 %all-to-all-done.2 = bf16[4,4,128,256]{3,1,2,0:T(4,128)(2,1)S(1)} async-done(((bf16[4,4,128,256]{3,1,2,0:T(4,128)(2,1)}), bf16[4,4,128,256]{3,1,2,0:T(4,128)(2,1)S(1)}, u32[]{:S(2)}, u32[]{:S(2)}) %all-to-all-start.2) | async-done | bytes 1048608 | tf_op jit(solution)/shard_map/all_to_all | solution.py:155
  112.1 0.2 copy.71
  112.3 0.7 convolution_convert_fusion.8
  112.9 0.4 fusion.28
  113.3 0.4 copy.74
  113.7 0.5 convolution_convert_fusion.2
  114.3 1.3 copy.75
  115.7 2.3 %fusion.74 = f32[2048,256]{1,0:T(8,128)S(1)} fusion(bf16[2048,512]{1,0:T(8,128)(2,1)} %all-gather.8.cloned.1.call-done, bf16[2,512,256]{2,1,0:T(8,128)(2,1)} %param.43), kind=kOutput, calls=%fused_computation.101 | convolution fusion | flops 536870912 | bytes 4456448 | tf_op jit(solution)/shard_map/dot_general | solution.py:34
  118.0 10.1 %all-gather.10.cloned.1.call-done = bf16[2048,512]{1,0:T(8,128)(2,1)} async-done(((bf16[2048,256]{1,0:T(8,128)(2,1)}), bf16[2048,512]{1,0:T(8,128)(2,1)}) %all-gather.10.cloned.1.call-update) | async-done | bytes 2097168 | tf_op jit(solution)/shard_map/all_gather | solution.py:47
  128.0 3.3 %fusion.20 = bf16[2048,256]{1,0:T(8,128)(2,1)} fusion(f32[2048,256]{1,0:T(8,128)S(1)} %fusion.74, bf16[2048,512]{1,0:T(8,128)(2,1)} %all-gather.10.cloned.1.call-done, bf16[2,512,256]{2,1,0:T(8,128)(2,1)} %param.43), kind=kOutput, calls=%fused_computation.30 | convolution fusion | flops 537919488 | bytes 5505024 | tf_op jit(solution)/shard_map/dot_general | solution.py:34
  131.3 11.7 %all-gather.12.cloned.1.call-done = bf16[2048,512]{1,0:T(8,128)(2,1)} async-done(((bf16[2048,256]{1,0:T(8,128)(2,1)}), bf16[2048,512]{1,0:T(8,128)(2,1)}) %all-gather.12.cloned.1.call-update) | async-done | bytes 2097168 | tf_op jit(solution)/shard_map/all_gather | solution.py:47
  143.0 2.1 %convert_reduce_fusion = f32[2048]{0:T(1024)S(1)} fusion(bf16[2048,512]{1,0:T(8,128)(2,1)} %all-gather.12.cloned.1.call-done), kind=kLoop, calls=%fused_computation.5 | loop fusion | flops 2095104 | bytes 2105344 | tf_op jit(solution)/shard_map/reduce_sum | solution.py:39
  145.1 0.1 copy-done.2
  145.2 1.0 fusion.4
  146.3 1.8 %convolution_bitcast_fusion = f32[1,1,2048,227]{2,3,1,0:T(8,128)S(1)} fusion(bf16[512,227]{0,1:T(8,128)(2,1)S(1)} %copy-done.15, bf16[2048,512]{1,0:T(8,128)(2,1)S(1)} %copy-done.2, f32[512]{0:T(512)S(1)} %copy-done.19, f32[2048]{0:T(1024)S(1)} %add_rsqrt_fusion, f32[2048]{0:T(1024)S(1)} %broadcast_multiply_fusion), kind=kOutput, calls=%fused_computation.29 | convolution fusion | flops 485490688 | bytes 4207616 | tf_op jit(solution)/shard_map/dot_general | solution.py:34
  148.1 3.1 %copy.76 = f32[1,1,2048,227]{2,1,3,0:T(1,128)} copy(f32[1,1,2048,227]{2,3,1,0:T(8,128)S(1)} %convolution_bitcast_fusion) | data formatting | bytes 3719168 | tf_op jit(solution)/shard_map/broadcast_in_dim | solution.py:169
  (83 shorter events, 1.0 us)
Async XLA Ops:
  6.5 1.2 copy-start
  6.5 3.6 %copy-start.20 = (s32[1,1,4]{2,1,0:T(1,128)S(1)}, s32[1,1,4]{2,1,0:T(1,128)}, u32[]{:S(2)}) copy-start(s32[1,1,4]{2,1,0:T(1,128)} %param.25) | copy-start | bytes 52
  6.5 4.6 %copy-start.21 = (s32[1,1,8]{2,1,0:T(1,128)S(1)}, s32[1,1,8]{2,1,0:T(1,128)}, u32[]{:S(2)}) copy-start(s32[1,1,8]{2,1,0:T(1,128)} %param.27) | copy-start | bytes 100
  6.5 10.0 %copy-start.10 = (s32[1,1,8]{2,1,0:T(1,128)S(1)}, s32[1,1,8]{2,1,0:T(1,128)}, u32[]{:S(2)}) copy-start(s32[1,1,8]{2,1,0:T(1,128)} %param.26) | copy-start | bytes 100
  6.5 15.8 %all-gather.6.cloned.1.call-start = ((), (), s32[]{:S(2)}) async-start(), calls=%async_computation.3 | async-start | bytes 3145728 | tf_op jit(solution)/shard_map/all_gather | solution.py:47
  12.0 19.1 %all-to-all-start = ((bf16[4,4,2]{1,2,0:T(2,128)(2,1)}), bf16[4,4,2]{1,2,0:T(2,128)(2,1)S(1)}, u32[]{:S(2)}, u32[]{:S(2)}) async-start(bf16[4,4,2]{1,2,0:T(2,128)(2,1)} %copy.62), calls=%async_computation | async-start | bytes 4096 | tf_op jit(solution)/shard_map/all_to_all | solution.py:124
  16.6 9.0 %copy-start.16 = (f32[512]{0:T(512)S(1)}, f32[512]{0:T(512)}, u32[]{:S(2)}) copy-start(f32[512]{0:T(512)} %param.35) | copy-start | bytes 6148
  22.3 2.2 %copy-start.1 = (bf16[2048,512]{1,0:T(8,128)(2,1)S(1)}, bf16[2048,512]{1,0:T(8,128)(2,1)}, u32[]{:S(2)}) copy-start(bf16[2048,512]{1,0:T(8,128)(2,1)} %all-gather.6.cloned.1.call-done) | copy-start | bytes 6291460
  22.3 3.3 %copy-start.12 = (bf16[512,256]{1,0:T(8,128)(2,1)S(1)}, bf16[512,256]{1,0:T(8,128)(2,1)}, u32[]{:S(2)}) copy-start(bf16[512,256]{1,0:T(8,128)(2,1)} %param.36) | copy-start | bytes 786436
  25.6 2.5 %copy-start.6 = (bf16[1,1,8,128,128]{4,3,2,1,0:T(8,128)(2,1)S(1)}, bf16[1,1,8,128,128]{4,3,2,1,0:T(8,128)(2,1)}, u32[]{:S(2)}) copy-start(bf16[1,1,8,128,128]{4,3,2,1,0:T(8,128)(2,1)} %param.28) | copy-start | bytes 786436
  27.5 1.0 copy-start.3
  29.8 6.0 %copy-start.9 = (bf16[1,1,256,256]{3,2,1,0:T(8,128)(2,1)S(1)}, bf16[1,1,256,256]{3,2,1,0:T(8,128)(2,1)}, u32[]{:S(2)}) copy-start(bf16[1,1,256,256]{3,2,1,0:T(8,128)(2,1)} %param.24) | copy-start | bytes 393220
  29.8 8.5 %copy-start.22 = (s32[1,1,2,1]{2,3,1,0:T(1,128)S(1)}, s32[1,1,2,1]{2,3,1,0:T(1,128)}, u32[]{:S(2)}) copy-start(s32[1,1,2,1]{2,3,1,0:T(1,128)} %param.32) | copy-start | bytes 28
  29.8 8.5 %copy-start.23 = (s32[1,1,8]{2,1,0:T(1,128)S(1)}, s32[1,1,8]{2,1,0:T(1,128)}, u32[]{:S(2)}) copy-start(s32[1,1,8]{2,1,0:T(1,128)} %param.29) | copy-start | bytes 100
  31.2 7.2 %copy-start.4 = (bf16[2,512,256]{2,1,0:T(8,128)(2,1)S(1)}, bf16[2,512,256]{2,1,0:T(8,128)(2,1)}, u32[]{:S(2)}) copy-start(bf16[2,512,256]{2,1,0:T(8,128)(2,1)} %param.37) | copy-start | bytes 1572868
  31.2 27.9 %all-to-all-start.1 = ((bf16[4,4,128,256]{3,1,2,0:T(4,128)(2,1)}), bf16[4,4,128,256]{3,1,2,0:T(4,128)(2,1)S(1)}, u32[]{:S(2)}, u32[]{:S(2)}) async-start(bf16[4,4,128,256]{3,1,2,0:T(4,128)(2,1)} %copy.65), calls=%async_computation.1 | async-start | bytes 2097152 | tf_op jit(solution)/shard_map/all_to_all | solution.py:123
  38.6 26.9 %copy-start.17 = (f32[512]{0:T(512)S(1)}, f32[512]{0:T(512)}, u32[]{:S(2)}) copy-start(f32[512]{0:T(512)} %param.38) | copy-start | bytes 6148
  59.1 6.4 %copy-start.13 = (bf16[512,256]{1,0:T(8,128)(2,1)S(1)}, bf16[512,256]{1,0:T(8,128)(2,1)}, u32[]{:S(2)}) copy-start(bf16[512,256]{1,0:T(8,128)(2,1)} %param.39) | copy-start | bytes 786436
  65.5 4.7 %copy-start.5 = (bf16[2,512,256]{2,1,0:T(8,128)(2,1)S(1)}, bf16[2,512,256]{2,1,0:T(8,128)(2,1)}, u32[]{:S(2)}) copy-start(bf16[2,512,256]{2,1,0:T(8,128)(2,1)} %param.40) | copy-start | bytes 1572868
  65.9 8.2 %copy-start.7 = (bf16[1,1,8,128,128]{4,3,2,1,0:T(8,128)(2,1)S(1)}, bf16[1,1,8,128,128]{4,3,2,1,0:T(8,128)(2,1)}, u32[]{:S(2)}) copy-start(bf16[1,1,8,128,128]{4,3,2,1,0:T(8,128)(2,1)} %param.31) | copy-start | bytes 786436
  68.7 3.2 %collective-permute-start.1 = (bf16[1,128,256]{2,1,0:T(8,128)(2,1)S(1)}, bf16[1,128,256]{2,1,0:T(8,128)(2,1)S(1)}, u32[]{:S(2)}, u32[]{:S(2)}) collective-permute-start(bf16[1,128,256]{2,1,0:T(8,128)(2,1)S(1)} %get-tuple-element.6), channel_id=1, source_target_pairs={{2,0},{0,2},{3,1},{1,3},{6,4},{4,6},{7,5},{5,7},{10,8},{8,10},{11,... | collective-permute-start | bytes 196616 | tf_op jit(solution)/shard_map/ppermute | solution.py:28
  69.9 3.5 %collective-permute-start = (bf16[1,128,256]{2,1,0:T(8,128)(2,1)S(1)}, bf16[1,128,256]{2,1,0:T(8,128)(2,1)S(1)}, u32[]{:S(2)}, u32[]{:S(2)}) collective-permute-start(bf16[1,128,256]{2,1,0:T(8,128)(2,1)S(1)} %get-tuple-element.5), channel_id=1, source_target_pairs={{0,2},{2,0},{1,3},{3,1},{4,6},{6,4},{5,7},{7,5},{8,10},{10,8},{9,1... | collective-permute-start | bytes 196616 | tf_op jit(solution)/shard_map/ppermute | solution.py:27
  70.5 4.4 %copy-start.11 = (s32[1,1,8]{2,1,0:T(1,128)S(1)}, s32[1,1,8]{2,1,0:T(1,128)}, u32[]{:S(2)}) copy-start(s32[1,1,8]{2,1,0:T(1,128)} %param.30) | copy-start | bytes 100
  74.5 6.4 %copy-start.14 = (bf16[512,256]{1,0:T(8,128)(2,1)S(1)}, bf16[512,256]{1,0:T(8,128)(2,1)}, u32[]{:S(2)}) copy-start(bf16[512,256]{1,0:T(8,128)(2,1)} %param.42) | copy-start | bytes 786436
  74.5 6.4 %copy-start.18 = (f32[512]{0:T(512)S(1)}, f32[512]{0:T(512)}, u32[]{:S(2)}) copy-start(f32[512]{0:T(512)} %param.41) | copy-start | bytes 6148
  83.1 29.0 %all-to-all-start.2 = ((bf16[4,4,128,256]{3,1,2,0:T(4,128)(2,1)}), bf16[4,4,128,256]{3,1,2,0:T(4,128)(2,1)S(1)}, u32[]{:S(2)}, u32[]{:S(2)}) async-start(bf16[4,4,128,256]{3,1,2,0:T(4,128)(2,1)} %convolution_convert_fusion.3), calls=%async_computation.2 | async-start | bytes 2097152 | tf_op jit(solution)/shard_map/all_to_all | solution.py:155
  88.7 27.0 %all-gather.8.cloned.1.call-start = ((), (), s32[]{:S(2)}) async-start(), calls=%async_computation.4 | async-start | bytes 3145728 | tf_op jit(solution)/shard_map/all_gather | solution.py:47
  89.4 23.5 %copy-start.8 = (bf16[1,1,8,128,128]{4,3,2,1,0:T(8,128)(2,1)S(1)}, bf16[1,1,8,128,128]{4,3,2,1,0:T(8,128)(2,1)}, u32[]{:S(2)}) copy-start(bf16[1,1,8,128,128]{4,3,2,1,0:T(8,128)(2,1)} %param.33) | copy-start | bytes 786436
  89.4 38.6 %all-gather.10.cloned.1.call-start = ((), (), s32[]{:S(2)}) async-start(), calls=%async_computation.5 | async-start | bytes 3145728 | tf_op jit(solution)/shard_map/all_gather | solution.py:47
  115.6 27.4 %all-gather.12.cloned.1.call-start = ((), (), s32[]{:S(2)}) async-start(), calls=%async_computation.6 | async-start | bytes 3145728 | tf_op jit(solution)/shard_map/all_gather | solution.py:47
  131.3 14.9 %copy-start.19 = (f32[512]{0:T(512)S(1)}, f32[512]{0:T(512)}, u32[]{:S(2)}) copy-start(f32[512]{0:T(512)} %param.44) | copy-start | bytes 6148
  143.0 2.2 %copy-start.2 = (bf16[2048,512]{1,0:T(8,128)(2,1)S(1)}, bf16[2048,512]{1,0:T(8,128)(2,1)}, u32[]{:S(2)}) copy-start(bf16[2048,512]{1,0:T(8,128)(2,1)} %all-gather.12.cloned.1.call-done) | copy-start | bytes 6291460
  143.0 3.3 %copy-start.15 = (bf16[512,227]{0,1:T(8,128)(2,1)S(1)}, bf16[512,227]{0,1:T(8,128)(2,1)}, u32[]{:S(2)}) copy-start(bf16[512,227]{0,1:T(8,128)(2,1)} %param.45) | copy-start | bytes 697348
Sparse Core Ops, SparseCore 0:
  10.3 12.0 all-gather.5
  91.0 11.7 all-gather.7
  115.7 12.2 all-gather.9
  131.4 11.5 all-gather.11
where the time goes:
time: 159 us; the launch traced here: 158 us
  waiting for transfers between devices  74.1 us (47%)
  matrix products  19.3 us (12%)
  starting transfers between devices  16.6 us (10%)
  blocking collectives  14.6 us (9%)
  between operations  13.7 us (9%)
  local copies, waits for them, and re-layouts  12 us (8%)
  other arithmetic  7.39 us (5%)
    all_gather x4, waiting for transfers between devices, widen(): lax.all_gather(as_sent(block_pieces), 'chan', axis=1, tiled=True)  27.4 us
    all_to_all x1, waiting for transfers between devices, local(): lax.all_to_all(answer, 'band', split_axis=0, concat_axis=0, tiled=True)  22.4 us
    all_to_all x1, waiting for transfers between devices, local(): lax.all_to_all(send_rows, 'band', split_axis=0, concat_axis=0, tiled=True)  20.5 us
    all_gather x6, blocking collectives, widen(): lax.all_gather(as_sent(block_pieces), 'chan', axis=1, tiled=True)  14.6 us
    dot_general x12, matrix products, matmul(): return jnp.dot(left, right, preferred_element_type=jnp.float32)  13.5 us
    all_to_all x1, starting transfers between devices, local(): lax.all_to_all(answer, 'band', split_axis=0, concat_axis=0, tiled=True)  5.58 us
    all_to_all x1, starting transfers between devices, local(): lax.all_to_all(send_rows, 'band', split_axis=0, concat_axis=0, tiled=True)  4.66 us
    all_to_all x1, starting transfers between devices, local(): lax.all_to_all(send_hot, 'band', split_axis=0, concat_axis=0, tiled=True)  4.53 us
  transfers between devices with their start and end apart: 9, of which 7 were waited for; matrix products, arithmetic and copies ran while one was open for 11% of the time, Pallas kernels for 0%

commit v1 on v0

v1 whole, which is shorter than its diff:
```python
import functools

import jax
import jax.numpy as jnp
from jax import lax
from jax.experimental import pallas as pl
from jax.experimental.pallas import tpu as pltpu
from jax.sharding import PartitionSpec as P

MESH = pl.DeviceIdType.MESH
F32 = jnp.float32
BF16 = jnp.bfloat16
M_BLK = 2


def mm(a, b):
    return jnp.dot(a, b, preferred_element_type=F32)


def norm_silu(v, gain):
    n = 1.0 / v.shape[-1]
    center = v - jnp.sum(v, axis=-1, keepdims=True) * n
    spread = jnp.sum(center * center, axis=-1, keepdims=True) * n
    half = center * lax.rsqrt(spread + 1e-5) * (0.5 * gain)
    return (half + half * jnp.tanh(half)).astype(BF16)


def front_kernel(
    B, S, E, PE,
    counts, esrc, etgt, psrc, ptgt, bound,
    x, eblk, pblk, ggain, egain, pgain,
    emb, gw1, gw2, ew1, ew2, pw1, pw2, dw1,
    base, mall, dsum_w,
    emb_f, gw1_f, gw2_f, ew1_f, ew2_f, pw1_f, pw2_f, dw1_f,
    lat, xs, own, psend, precv, half_send, half_recv, m1, bsend, srcs, wide,
    loc_sem, wsend_sem, wrecv_sem, as_sem, ar_sem, hs_sem, hr_sem, bs_sem, br_sem,
    gs_sem, gr_sem, fs_sem, fr_sem,
):
    me = lax.axis_index("band")
    sec = lax.axis_index("sector")
    c = lax.axis_index("chan")
    oc = 1 - c
    hw = gw2.shape[-1]
    nxt = lax.rem(sec + 1, S)
    prv = lax.rem(sec + S - 1, S)
    mrows = emb.shape[0]
    rows = mrows // M_BLK
    g_blk = lat.shape[1]
    cols = pl.ds(pl.multiple_of(c * hw, hw), hw)
    ocols = pl.ds(pl.multiple_of(oc * hw, hw), hw)

    parts = [
        (gw1, gw1_f.at[:, cols]),
        (gw2, gw2_f.at[:, cols]),
        (emb, emb_f.at[:, cols]),
        (ew1, ew1_f.at[:, :, cols]),
        (dw1.at[0], dw1_f.at[:, cols]),
        (ew2, ew2_f.at[:, cols]),
        (pw1, pw1_f.at[:, :, cols]),
        (pw2, pw2_f.at[:, cols]),
        (dw1.at[1], dsum_w.at[:, cols]),
    ]
    local = [pltpu.make_async_copy(s, d, loc_sem.at[i]) for i, (s, d) in enumerate(parts)]
    for cp in local:
        cp.start()

    barrier = pltpu.get_barrier_semaphore()
    pl.semaphore_signal(barrier, inc=1, device_id={"chan": oc}, device_id_type=MESH)
    pl.semaphore_signal(barrier, inc=1, device_id={"sector": nxt}, device_id_type=MESH)
    pl.semaphore_signal(barrier, inc=1, device_id={"sector": prv}, device_id_type=MESH)
    for d in range(1, B):
        pl.semaphore_signal(
            barrier, inc=1, device_id={"band": lax.rem(me + d, B)}, device_id_type=MESH
        )
    pl.semaphore_wait(barrier, B + 2)

    remote = [
        pltpu.make_async_remote_copy(
            s, d, wsend_sem.at[i], wrecv_sem.at[i], device_id={"chan": oc}, device_id_type=MESH
        )
        for i, (s, d) in enumerate(parts)
    ]
    for cp in remote:
        cp.start()

    def arrived(i):
        local[i].wait()
        remote[i].wait_recv()

    arrived(0)
    arrived(1)

    chunk = 2 * rows

    def grid_step(i, _):
        r = pl.ds(pl.multiple_of(i * chunk, chunk), chunk)
        h = norm_silu(mm(x[r, :], gw1_f[...]), ggain[...])
        latent = mm(h, gw2_f[...]).astype(BF16)
        for k in range(2):
            for j in range(2):
                lat[k, 2 * i + j] = latent[j * rows : (j + 1) * rows, k * hw : (k + 1) * hw]
        return 0

    lax.fori_loop(0, g_blk // 2, grid_step, 0, unroll=2)

    for e in range(E):
        xs[e * rows : (e + 1) * rows, :] = lat[c, esrc[e]]

    def part_for(q):
        lo = jnp.int32(0)
        size = jnp.int32(0)
        for p in range(B):
            lo = lo + jnp.where(p < q, counts[p], 0)
            size = size + jnp.where(p == q, counts[p], 0)
        acc = []
        for m in range(M_BLK):
            pieces = []
            for e in range(E):
                keep = jnp.where((lo <= e) & (e < lo + size) & (etgt[e] == m), 1.0, 0.0)
                pieces.append(eblk[e] * keep.astype(BF16))
            acc.append(mm(jnp.concatenate(pieces, axis=1), xs[...]))
        return acc

    def band_copy(d):
        return pltpu.make_async_remote_copy(
            psend.at[d - 1], precv.at[d - 1], as_sem.at[d - 1], ar_sem.at[d - 1],
            device_id={"band": lax.rem(me + d, B)}, device_id_type=MESH,
        )

    def send_step(d, _):
        acc = part_for(lax.rem(me + d, B))
        for m in range(M_BLK):
            psend[d - 1, m * rows : (m + 1) * rows, :] = acc[m].astype(BF16)
        band_copy(d).start()
        return 0

    lax.fori_loop(1, B, send_step, 0, unroll=B <= 4)
    acc = part_for(me)
    for m in range(M_BLK):
        own[m * rows : (m + 1) * rows, :] = acc[m]

    arrived(2)
    arrived(3)
    wide[...] = mm(emb_f[...], ew1_f[0])
    arrived(4)

    def base_step(i, _):
        left = jnp.concatenate([lat[0, 2 * i], lat[0, 2 * i + 1]], axis=0)
        right = jnp.concatenate([lat[1, 2 * i], lat[1, 2 * i + 1]], axis=0)
        out = mm(left, dw1_f[:hw, :]) + mm(right, dw1_f[hw:, :])
        base[pl.ds(pl.multiple_of(i * chunk, chunk), chunk), :] = out.astype(BF16)
        return 0

    lax.fori_loop(0, g_blk // 2, base_step, 0)

    def take_step(d, _):
        band_copy(d).wait_recv()
        own[...] += precv[d - 1].astype(F32)
        return 0

    lax.fori_loop(1, B, take_step, 0, unroll=B <= 4)

    def update(k, summed, w1, gain, w2):
        half_send[k] = summed.astype(BF16)
        cp = pltpu.make_async_remote_copy(
            half_send.at[k], half_recv.at[k], hs_sem.at[k], hr_sem.at[k],
            device_id={"chan": oc}, device_id_type=MESH,
        )
        cp.start()
        pre = wide[...] + mm(half_send[k], w1[1, cols, :])
        cp.wait_recv()
        pre = pre + mm(half_recv[k], w1[1, ocols, :])
        cp.wait_send()
        return mm(norm_silu(pre, gain[...]), w2[...])

    arrived(5)
    one = (emb_f[...].astype(F32) + update(0, own[...], ew1_f, egain, ew2_f)).astype(BF16)
    for k in range(2):
        for j in range(M_BLK):
            m1[k, j] = one[j * rows : (j + 1) * rows, k * hw : (k + 1) * hw]
    bsend[0] = m1[c, bound[0]]
    bsend[1] = m1[c, bound[1]]
    to_next = pltpu.make_async_remote_copy(
        bsend.at[1], srcs.at[M_BLK], bs_sem.at[1], br_sem.at[0],
        device_id={"sector": nxt}, device_id_type=MESH,
    )
    to_prev = pltpu.make_async_remote_copy(
        bsend.at[0], srcs.at[M_BLK + 1], bs_sem.at[0], br_sem.at[1],
        device_id={"sector": prv}, device_id_type=MESH,
    )
    to_next.start()
    to_prev.start()
    for j in range(M_BLK):
        srcs[j] = m1[c, j]
    arrived(6)
    wide[...] = mm(one, pw1_f[0])
    to_next.wait_recv()
    to_prev.wait_recv()
    ys = jnp.concatenate([srcs[psrc[e]] for e in range(PE)], axis=0)
    for m in range(M_BLK):
        pieces = []
        for e in range(PE):
            keep = jnp.where(ptgt[e] == m, 1.0, 0.0)
            pieces.append(pblk[e] * keep.astype(BF16))
        own[m * rows : (m + 1) * rows, :] = mm(jnp.concatenate(pieces, axis=1), ys)
    arrived(7)
    two = (one.astype(F32) + update(1, own[...], pw1_f, pgain, pw2_f)).astype(BF16)
    for k in range(2):
        mall[k, me] = two[:, k * hw : (k + 1) * hw]

    def out_copy(d):
        return pltpu.make_async_remote_copy(
            mall.at[c, me], mall.at[c, me], gs_sem.at[d - 1], gr_sem.at[d - 1],
            device_id={"band": lax.rem(me + d, B)}, device_id_type=MESH,
        )

    def in_copy(d):
        src = lax.rem(me - d + B, B)
        return pltpu.make_async_remote_copy(
            mall.at[c, src], mall.at[c, src], gs_sem.at[d - 1], gr_sem.at[d - 1],
            device_id={"band": lax.rem(me + d, B)}, device_id_type=MESH,
        )

    def forward(d, half):
        src = lax.rem(me - d + B, B)
        return pltpu.make_async_remote_copy(
            mall.at[half, src], mall.at[half, src], fs_sem.at[d - 1], fr_sem.at[d - 1],
            device_id={"chan": oc}, device_id_type=MESH,
        )

    def gather_start(d, _):
        out_copy(d).start()
        return 0

    def gather_pass(d, _):
        in_copy(d).wait_recv()
        forward(d, c).start()
        return 0

    def gather_end(d, _):
        forward(d, oc).wait_recv()
        forward(d, c).wait_send()
        out_copy(d).wait_send()
        band_copy(d).wait_send()
        return 0

    lax.fori_loop(1, B, gather_start, 0, unroll=B <= 4)
    arrived(8)
    to_next.wait_send()
    to_prev.wait_send()
    for cp in remote:
        cp.wait_send()
    lax.fori_loop(1, B, gather_pass, 0, unroll=B <= 4)
    lax.fori_loop(1, B, gather_end, 0, unroll=B <= 4)


def back_kernel(B, E, counts, esrc, etgt, base, mall, dsum_w, dblk, dgain, dw2, out, acc):
    rows = dblk.shape[1]
    g_blk = acc.shape[0]
    hw = mall.shape[-1]
    for g in range(g_blk):
        acc[g] = base[g * rows : (g + 1) * rows, :].astype(F32)

    def edge(e, _):
        peer = jnp.int32(0)
        end = jnp.int32(0)
        for p in range(B):
            end = end + counts[p]
            peer = peer + jnp.where(end <= e, 1, 0)
        r = pl.ds(pl.multiple_of(etgt[e] * rows, rows), rows)
        add = jnp.zeros((rows, 2 * hw), F32)
        for k in range(2):
            msg = mm(dblk[e], mall[k, peer, r, :]).astype(BF16)
            add = add + mm(msg, dsum_w[k * hw : (k + 1) * hw, :])
        acc[esrc[e]] += add
        return 0

    lax.fori_loop(0, E, edge, 0, unroll=4)

    def final(i, _):
        v = jnp.concatenate([acc[2 * i], acc[2 * i + 1]], axis=0)
        h = norm_silu(v, dgain[...])
        out[pl.ds(pl.multiple_of(i * 2 * rows, 2 * rows), 2 * rows), :] = mm(h, dw2[...])
        return 0

    lax.fori_loop(0, g_blk // 2, final, 0, unroll=2)


def local(
    grid_inputs, emb, counts, esrc, etgt, eblk, psrc, ptgt, pblk, bound, dblk,
    gw1, ggain, gw2, ew1, egain, ew2, pw1, pgain, pw2, dw1, dgain, dw2, B, S,
):
    E = eblk.shape[2]
    PE = pblk.shape[2]
    rows = eblk.shape[-1]
    n, ch = grid_inputs.shape[2:]
    mrows, hw = emb.shape[2:]
    lat_w = 2 * hw
    g_blk = n // rows
    smem = pl.BlockSpec(memory_space=pltpu.SMEM)
    vmem = pl.BlockSpec(memory_space=pltpu.VMEM)
    hbm = pl.BlockSpec(memory_space=pl.ANY)
    dma = pltpu.SemaphoreType.DMA
    base, mall, dsum_w = pl.pallas_call(
        functools.partial(front_kernel, B, S, E, PE),
        out_shape=(
            jax.ShapeDtypeStruct((n, lat_w), BF16),
            jax.ShapeDtypeStruct((2, B, mrows, hw), BF16),
            jax.ShapeDtypeStruct((lat_w, lat_w), BF16),
        ),
        in_specs=[smem] * 6 + [vmem] * 6 + [hbm] * 8,
        out_specs=(vmem, vmem, vmem),
        scratch_shapes=[
            pltpu.VMEM((mrows, lat_w), BF16),
            pltpu.VMEM((ch, lat_w), BF16),
            pltpu.VMEM((lat_w, lat_w), BF16),
            pltpu.VMEM((2, lat_w, lat_w), BF16),
            pltpu.VMEM((lat_w, lat_w), BF16),
            pltpu.VMEM((2, lat_w, lat_w), BF16),
            pltpu.VMEM((lat_w, lat_w), BF16),
            pltpu.VMEM((lat_w, lat_w), BF16),
            pltpu.VMEM((2, g_blk, rows, hw), BF16),
            pltpu.VMEM((E * rows, hw), BF16),
            pltpu.VMEM((mrows, hw), F32),
            pltpu.VMEM((B - 1, mrows, hw), BF16),
            pltpu.VMEM((B - 1, mrows, hw), BF16),
            pltpu.VMEM((2, mrows, hw), BF16),
            pltpu.VMEM((2, mrows, hw), BF16),
            pltpu.VMEM((2, M_BLK, rows, hw), BF16),
            pltpu.VMEM((2, rows, hw), BF16),
            pltpu.VMEM((M_BLK + 2, rows, hw), BF16),
            pltpu.VMEM((mrows, lat_w), F32),
            dma((9,)), dma((9,)), dma((9,)),
            dma((B - 1,)), dma((B - 1,)),
            dma((2,)), dma((2,)), dma((2,)), dma((2,)),
            dma((B - 1,)), dma((B - 1,)), dma((B - 1,)), dma((B - 1,)),
        ],
        compiler_params=pltpu.CompilerParams(
            collective_id=0, has_side_effects=True, vmem_limit_bytes=48 * 2**20
        ),
    )(
        counts[0, 0], esrc[0, 0], etgt[0, 0], psrc[0, 0], ptgt[0, 0], bound.reshape(-1),
        grid_inputs[0, 0], eblk[0, 0], pblk[0, 0],
        ggain.reshape(1, -1), egain.reshape(1, -1), pgain.reshape(1, -1),
        emb[0, 0], gw1, gw2, ew1, ew2, pw1, pw2, dw1,
    )
    out = pl.pallas_call(
        functools.partial(back_kernel, B, E),
        out_shape=jax.ShapeDtypeStruct((n, ch), F32),
        in_specs=[smem] * 3 + [vmem] * 6,
        out_specs=vmem,
        scratch_shapes=[pltpu.VMEM((g_blk, rows, lat_w), F32)],
        compiler_params=pltpu.CompilerParams(vmem_limit_bytes=48 * 2**20),
    )(
        counts[0, 0], esrc[0, 0], etgt[0, 0],
        base, mall, dsum_w, dblk[0, 0], dgain.reshape(1, -1), dw2,
    )
    return out[None, None]


def solution(mesh):
    B, S = mesh.shape["band"], mesh.shape["sector"]
    idx = P("band", "sector", None)
    blk = P("band", "sector", None, None, None)
    rows = P(("groups", "band"), "sector", None, None)
    w3 = P(None, None, "chan")
    w2 = P(None, "chan")
    in_specs = (
        rows, P(("groups", "band"), "sector", None, "chan"),
        idx, idx, idx, blk, idx, idx, blk, P("band", "sector", None, None), blk,
        w2, P(), w2, w3, P(), w2, w3, P(), w2, w3, P(), P(),
    )
    return jax.shard_map(
        functools.partial(local, B=B, S=S),
        mesh=mesh, in_specs=in_specs, out_specs=rows, check_vma=False,
    )
```

time: 159 us -> 68.4 us (0.43)
  waiting for transfers between devices: 74.1 us -> 0 us
  Pallas kernels: 0 us -> 54.6 us
  matrix products: 19.3 us -> 0 us
  starting transfers between devices: 16.6 us -> 0 us
  blocking collectives: 14.6 us -> 0 us
  between operations: 13.7 us -> 0.2 us
  other arithmetic: 7.39 us -> 0 us
    pallas_call x0 -> x2, Pallas kernels: none -> 54.6 us  [the longest x1 48.5 us: local(): pl.pallas_call(functools.partial(front_kernel, B, S, E, PE), out_shape=(j...]
    all_to_all x3 -> x0, waiting for transfers between devices: 42.9 us -> none  [the longest x1 22.4 us: local(): lax.all_to_all(answer, 'band', split_axis=0, concat_axis=0, tiled=True)]
    all_gather x4 -> x0, waiting for transfers between devices: 27.4 us -> none  [widen(): lax.all_gather(as_sent(block_pieces), 'chan', axis=1, tiled=True)]
    dot_general x21 -> x0, matrix products: 19.3 us -> none  [the longest x12 13.5 us: matmul(): return jnp.dot(left, right, preferred_element_type=jnp.float32)]
    all_to_all x3 -> x0, starting transfers between devices: 14.8 us -> none  [the longest x1 5.58 us: local(): lax.all_to_all(answer, 'band', split_axis=0, concat_axis=0, tiled=True)]
    all_gather x6 -> x0, blocking collectives: 14.6 us -> none  [widen(): lax.all_gather(as_sent(block_pieces), 'chan', axis=1, tiled=True)]
    unnamed x48 -> x44, local copies, waits for them, and re-layouts: 1.49 us -> 9.74 us
    reduce_sum x9 -> x0, other arithmetic: 6.97 us -> none  [the longest x4 4.4 us: norm_silu(): center = values - jnp.mean(values, axis=-1, keepdims=True)]
  transfers between devices with their start and end apart: 9 -> 0, of which waited for: 7 -> 0; matrix products, arithmetic and copies ran while one was open for 11% -> 0% of each run, Pallas kernels for 0% -> 0%
where the time goes in v1:
time: 68.4 us; the launch traced here: 68.1 us
  Pallas kernels  54.6 us (80%)
  local copies, waits for them, and re-layouts  13.3 us (19%)
    pallas_call x1, Pallas kernels, local(): pl.pallas_call(functools.partial(front_kernel, B, S, E, PE), out_shape=(j...  48.5 us
    unnamed x44, local copies, waits for them, and re-layouts  9.74 us
    pallas_call x1, Pallas kernels, local(): pl.pallas_call(functools.partial(back_kernel, B, E), out_shape=jax.ShapeD...  6.09 us
    broadcast_in_dim x1, local copies, waits for them, and re-layouts, local(): return out[None, None]  3.56 us

profile of v1, /device:TPU:25, one launch (start us, length us, event | category | flops | bytes accessed | tf_op | source)
XLA Modules:
  0.0 68.1 jit_solution(9765173048572120998)
XLA Ops:
  0.0 0.0 copy-start.2
  0.0 0.0 copy-start.14
  0.0 0.0 copy-start.1
  0.0 0.0 copy-start.13
  0.0 0.0 copy-start
  0.0 0.0 copy-start.12
  0.0 0.0 copy-start.5
  0.0 0.0 copy-start.4
  0.1 0.0 copy-start.15
  0.1 0.0 copy-start.9
  0.1 1.2 %copy.25.dw2 = bf16[512,227]{1,0:T(8,128)(2,1)S(1)} copy(bf16[512,227]{0,1:T(8,128)(2,1)} %param.45) | data formatting | bytes 464896 | tf_op args[22]
  1.3 1.5 %copy.24 = bf16[1,1,2048,227]{3,2,1,0:T(8,128)(2,1)S(1)} copy(bf16[1,1,2048,227]{2,3,1,0:T(8,128)(2,1)} %param.23) | data formatting | bytes 1859584 | tf_op args[0]
  2.8 0.0 copy-done.2
  2.8 0.0 copy-done.14
  2.8 0.0 copy-done.1
  2.8 0.0 copy-done.13
  2.8 0.0 copy-done
  2.8 0.0 copy-done.12
  2.8 0.0 copy-done.5
  2.8 0.0 copy-done.4
  2.9 0.0 copy-done.15
  2.9 0.0 copy-done.9
  2.9 0.0 copy-start.6
  2.9 0.9 %copy-done.6 = bf16[512,256]{1,0:T(8,128)(2,1)S(1)} copy-done((bf16[512,256]{1,0:T(8,128)(2,1)S(1)}, bf16[512,256]{1,0:T(8,128)(2,1)}, u32[]{:S(2)}) %copy-start.6) | copy-done | bytes 262168
  3.8 0.0 copy-start.7
  3.8 0.9 %copy-done.7 = bf16[512,256]{1,0:T(8,128)(2,1)S(1)} copy-done((bf16[512,256]{1,0:T(8,128)(2,1)S(1)}, bf16[512,256]{1,0:T(8,128)(2,1)}, u32[]{:S(2)}) %copy-start.7) | copy-done | bytes 262168
  4.8 0.0 copy-start.8
  4.8 0.9 %copy-done.8 = bf16[512,256]{1,0:T(8,128)(2,1)S(1)} copy-done((bf16[512,256]{1,0:T(8,128)(2,1)S(1)}, bf16[512,256]{1,0:T(8,128)(2,1)}, u32[]{:S(2)}) %copy-start.8) | copy-done | bytes 262168
  5.7 0.0 copy-start.10
  5.7 0.9 %copy-done.10 = bf16[227,256]{1,0:T(8,128)(2,1)S(1)} copy-done((bf16[227,256]{1,0:T(8,128)(2,1)S(1)}, bf16[227,256]{1,0:T(8,128)(2,1)}, u32[]{:S(2)}) %copy-start.10) | copy-done | bytes 116248
  6.6 0.0 copy-start.16
  6.6 0.7 copy-done.16
  7.3 0.0 copy-start.17
  7.3 0.7 copy-done.17
  7.9 0.0 copy-start.18
  7.9 0.7 copy-done.18
  8.6 0.0 copy-start.19
  8.6 0.7 copy-done.19
  9.3 0.0 copy-start.20
  9.3 0.7 copy-done.20
  9.9 0.0 copy-start.3
  9.9 0.0 copy-start.11
  9.9 48.5 %shard_map.217 = (bf16[2048,512]{1,0:T(8,128)(2,1)}, bf16[2,4,256,256]{3,2,1,0:T(8,128)(2,1)S(1)}, bf16[512,512]{1,0:T(8,128)(2,1)S(1)}) custom-call(s32[4]{0:T(128)S(1)} %bitcast.26, s32[8]{0:T(128)S(1)} %bitcast.28, s32[8]{0:T(128)S(1)} %bitcast.30, s32[8]{0:T(128)S(1)} %bitcast.32, s32[8]{0:T(128)S(1)} %bitcast.33, s32[2]{0:T(128)S(1)} %bitcast.34, ...), custom_call_target="tpu_custom_call" | custom-call | tf_op jit(solution)/shard_map/pallas_call | solution.py:304
  58.4 0.0 copy-done.3
  58.4 0.0 copy-done.11
  58.4 6.1 %shard_map.218 = f32[2048,227]{1,0:T(8,128)S(1)} custom-call(s32[4]{0:T(128)S(1)} %bitcast.27, s32[8]{0:T(128)S(1)} %bitcast.29, s32[8]{0:T(128)S(1)} %bitcast.31, bf16[2048,512]{1,0:T(8,128)(2,1)} %get-tuple-element.8.base, bf16[2,4,256,256]{3,2,1,0:T(8,128)(2,1)S(1)} %get-tuple-element.9.mall, bf16[512,512]{1,0:T(8,128)(2,1)S(1)} %get-tuple-element.10.dsum_w, ...), custom_call_target="tpu_custom_call" | custom-call | tf_op jit(solution)/shard_map/pallas_call | solution.py:347
  64.5 3.6 %copy.26 = f32[1,1,2048,227]{2,1,3,0:T(1,128)} copy(f32[1,1,2048,227]{3,2,1,0:T(8,128)S(1)} %bitcast.16) | data formatting | bytes 3719168 | tf_op jit(solution)/shard_map/broadcast_in_dim | solution.py:358
Async XLA Ops:
  0.0 2.8 %copy-start.2 = (bf16[2,512,256]{2,1,0:T(8,128)(2,1)S(1)}, bf16[2,512,256]{2,1,0:T(8,128)(2,1)}, u32[]{:S(2)}) copy-start(bf16[2,512,256]{2,1,0:T(8,128)(2,1)} %dw1.1) | copy-start | bytes 1572868
  0.0 2.8 %copy-start.14 = (f32[512]{0:T(512)S(1)}, f32[512]{0:T(512)}, u32[]{:S(2)}) copy-start(f32[512]{0:T(512)} %param.41) | copy-start | bytes 6148
  0.0 2.8 %copy-start.1 = (bf16[2,512,256]{2,1,0:T(8,128)(2,1)S(1)}, bf16[2,512,256]{2,1,0:T(8,128)(2,1)}, u32[]{:S(2)}) copy-start(bf16[2,512,256]{2,1,0:T(8,128)(2,1)} %pw1.1) | copy-start | bytes 1572868
  0.0 2.8 %copy-start.13 = (f32[512]{0:T(512)S(1)}, f32[512]{0:T(512)}, u32[]{:S(2)}) copy-start(f32[512]{0:T(512)} %param.38) | copy-start | bytes 6148
  0.0 2.8 %copy-start = (bf16[2,512,256]{2,1,0:T(8,128)(2,1)S(1)}, bf16[2,512,256]{2,1,0:T(8,128)(2,1)}, u32[]{:S(2)}) copy-start(bf16[2,512,256]{2,1,0:T(8,128)(2,1)} %ew1.1) | copy-start | bytes 1572868
  0.0 2.8 %copy-start.12 = (f32[512]{0:T(512)S(1)}, f32[512]{0:T(512)}, u32[]{:S(2)}) copy-start(f32[512]{0:T(512)} %param.35) | copy-start | bytes 6148
  0.0 2.8 %copy-start.5 = (bf16[1,1,8,128,128]{4,3,2,1,0:T(8,128)(2,1)S(1)}, bf16[1,1,8,128,128]{4,3,2,1,0:T(8,128)(2,1)}, u32[]{:S(2)}) copy-start(bf16[1,1,8,128,128]{4,3,2,1,0:T(8,128)(2,1)} %param.31) | copy-start | bytes 786436
  0.0 2.8 %copy-start.4 = (bf16[1,1,8,128,128]{4,3,2,1,0:T(8,128)(2,1)S(1)}, bf16[1,1,8,128,128]{4,3,2,1,0:T(8,128)(2,1)}, u32[]{:S(2)}) copy-start(bf16[1,1,8,128,128]{4,3,2,1,0:T(8,128)(2,1)} %param.28) | copy-start | bytes 786436
  0.1 2.8 %copy-start.15 = (s32[1,1,4]{2,1,0:T(1,128)S(1)}, s32[1,1,4]{2,1,0:T(1,128)}, u32[]{:S(2)}) copy-start(s32[1,1,4]{2,1,0:T(1,128)} %param.25) | copy-start | bytes 52
  0.1 2.8 %copy-start.9 = (bf16[1,1,256,256]{3,2,1,0:T(8,128)(2,1)S(1)}, bf16[1,1,256,256]{3,2,1,0:T(8,128)(2,1)}, u32[]{:S(2)}) copy-start(bf16[1,1,256,256]{3,2,1,0:T(8,128)(2,1)} %param.24) | copy-start | bytes 393220
  2.9 1.0 %copy-start.6 = (bf16[512,256]{1,0:T(8,128)(2,1)S(1)}, bf16[512,256]{1,0:T(8,128)(2,1)}, u32[]{:S(2)}) copy-start(bf16[512,256]{1,0:T(8,128)(2,1)} %gw2.1) | copy-start | bytes 786436
  3.8 0.9 %copy-start.7 = (bf16[512,256]{1,0:T(8,128)(2,1)S(1)}, bf16[512,256]{1,0:T(8,128)(2,1)}, u32[]{:S(2)}) copy-start(bf16[512,256]{1,0:T(8,128)(2,1)} %ew2.1) | copy-start | bytes 786436
  4.8 0.9 %copy-start.8 = (bf16[512,256]{1,0:T(8,128)(2,1)S(1)}, bf16[512,256]{1,0:T(8,128)(2,1)}, u32[]{:S(2)}) copy-start(bf16[512,256]{1,0:T(8,128)(2,1)} %pw2.1) | copy-start | bytes 786436
  5.7 0.9 %copy-start.10 = (bf16[227,256]{1,0:T(8,128)(2,1)S(1)}, bf16[227,256]{1,0:T(8,128)(2,1)}, u32[]{:S(2)}) copy-start(bf16[227,256]{1,0:T(8,128)(2,1)} %gw1.1) | copy-start | bytes 348676
  6.6 0.7 copy-start.16
  7.3 0.7 copy-start.17
  7.9 0.7 copy-start.18
  8.6 0.7 copy-start.19
  9.3 0.7 copy-start.20
  9.9 48.5 %copy-start.3 = (bf16[1,1,8,128,128]{4,3,2,1,0:T(8,128)(2,1)S(1)}, bf16[1,1,8,128,128]{4,3,2,1,0:T(8,128)(2,1)}, u32[]{:S(2)}) copy-start(bf16[1,1,8,128,128]{4,3,2,1,0:T(8,128)(2,1)} %param.33) | copy-start | bytes 786436
  9.9 48.5 %copy-start.11 = (f32[512]{0:T(512)S(1)}, f32[512]{0:T(512)}, u32[]{:S(2)}) copy-start(f32[512]{0:T(512)} %param.44) | copy-start | bytes 6148

commit v2 on v1

--- a/solution.py
+++ b/solution.py
@@ -94,7 +94,10 @@
 
     def grid_step(i, _):
         r = pl.ds(pl.multiple_of(i * chunk, chunk), chunk)
-        h = norm_silu(mm(x[r, :], gw1_f[...]), ggain[...])
+        pre = lax.dot_general(
+            x[:, r], gw1_f[...], (((0,), (0,)), ((), ())), preferred_element_type=F32
+        )
+        h = norm_silu(pre, ggain[...])
         latent = mm(h, gw2_f[...]).astype(BF16)
         for k in range(2):
             for j in range(2):
@@ -280,7 +283,10 @@
     def final(i, _):
         v = jnp.concatenate([acc[2 * i], acc[2 * i + 1]], axis=0)
         h = norm_silu(v, dgain[...])
-        out[pl.ds(pl.multiple_of(i * 2 * rows, 2 * rows), 2 * rows), :] = mm(h, dw2[...])
+        r = pl.ds(pl.multiple_of(i * 2 * rows, 2 * rows), 2 * rows)
+        out[:, 0, r] = lax.dot_general(
+            dw2[...], h, (((1,), (1,)), ((), ())), preferred_element_type=F32
+        )
         return 0
 
     lax.fori_loop(0, g_blk // 2, final, 0, unroll=2)
@@ -336,26 +342,26 @@
             dma((B - 1,)), dma((B - 1,)), dma((B - 1,)), dma((B - 1,)),
         ],
         compiler_params=pltpu.CompilerParams(
-            collective_id=0, has_side_effects=True, vmem_limit_bytes=48 * 2**20
+            collective_id=0, has_side_effects=True, vmem_limit_bytes=63 * 2**20
         ),
     )(
         counts[0, 0], esrc[0, 0], etgt[0, 0], psrc[0, 0], ptgt[0, 0], bound.reshape(-1),
-        grid_inputs[0, 0], eblk[0, 0], pblk[0, 0],
+        grid_inputs[0, 0].T, eblk[0, 0], pblk[0, 0],
         ggain.reshape(1, -1), egain.reshape(1, -1), pgain.reshape(1, -1),
         emb[0, 0], gw1, gw2, ew1, ew2, pw1, pw2, dw1,
     )
     out = pl.pallas_call(
         functools.partial(back_kernel, B, E),
-        out_shape=jax.ShapeDtypeStruct((n, ch), F32),
+        out_shape=jax.ShapeDtypeStruct((ch, 1, n), F32),
         in_specs=[smem] * 3 + [vmem] * 6,
         out_specs=vmem,
         scratch_shapes=[pltpu.VMEM((g_blk, rows, lat_w), F32)],
-        compiler_params=pltpu.CompilerParams(vmem_limit_bytes=48 * 2**20),
+        compiler_params=pltpu.CompilerParams(vmem_limit_bytes=63 * 2**20),
     )(
         counts[0, 0], esrc[0, 0], etgt[0, 0],
-        base, mall, dsum_w, dblk[0, 0], dgain.reshape(1, -1), dw2,
-    )
-    return out[None, None]
+        base, mall, dsum_w, dblk[0, 0], dgain.reshape(1, -1), dw2.T,
+    )
+    return jnp.transpose(out, (1, 2, 0))[None]
 
 
 def solution(mesh):

time: 68.4 us -> 58.6 us (0.86)
  local copies, waits for them, and re-layouts: 13.3 us -> 0 us
  Pallas kernels: 54.6 us -> 58.4 us
    unnamed x44 -> x0, local copies, waits for them, and re-layouts: 9.74 us -> none
    broadcast_in_dim x1 -> x0, local copies, waits for them, and re-layouts: 3.56 us -> none  [local(): return out[None, None]]
    pallas_call x1, Pallas kernels: 6.09 us -> 8.59 us  [local(): pl.pallas_call(functools.partial(back_kernel, B, E), out_shape=jax.ShapeD...]
    pallas_call x1, Pallas kernels: 48.5 us -> 49.8 us  [local(): pl.pallas_call(functools.partial(front_kernel, B, S, E, PE), out_shape=(j...]
where the time goes in v2:
time: 58.6 us; the launch traced here: 58.4 us
  Pallas kernels  58.4 us (100%)
    pallas_call x1, Pallas kernels, local(): pl.pallas_call(functools.partial(front_kernel, B, S, E, PE), out_shape=(j...  49.8 us
    pallas_call x1, Pallas kernels, local(): pl.pallas_call(functools.partial(back_kernel, B, E), out_shape=jax.ShapeD...  8.59 us

profile of v2, /device:TPU:25, one launch (start us, length us, event | category | flops | bytes accessed | tf_op | source)
XLA Modules:
  0.0 58.4 jit_solution(14453265121982893885)
XLA Ops:
  0.0 49.8 %shard_map.217 = (bf16[2048,512]{1,0:T(8,128)(2,1)}, bf16[2,4,256,256]{3,2,1,0:T(8,128)(2,1)}, bf16[512,512]{1,0:T(8,128)(2,1)}) custom-call(s32[4]{0:T(128)} %bitcast.33, s32[8]{0:T(128)} %bitcast.35, s32[8]{0:T(128)} %bitcast.37, s32[8]{0:T(128)} %bitcast.39, s32[8]{0:T(128)} %bitcast.40, s32[2]{0:T(128)} %bitcast.41, bf16[227,2048]{1,0:T(8,128)(2,1)} %bitcast.23, ...), custom_call_target="tpu_custom_call" | custom-call | tf_op jit(solution)/shard_map/pallas_call | solution.py:310
  49.9 8.6 %shard_map.218 = f32[227,1,2048]{2,1,0:T(1,128)} custom-call(s32[4]{0:T(128)} %bitcast.34, s32[8]{0:T(128)} %bitcast.36, s32[8]{0:T(128)} %bitcast.38, bf16[2048,512]{1,0:T(8,128)(2,1)} %get-tuple-element.8.base, bf16[2,4,256,256]{3,2,1,0:T(8,128)(2,1)} %get-tuple-element.9.mall, bf16[512,512]{1,0:T(8,128)(2,1)} %get-tuple-element.10.dsum_w, ...), custom_call_target="tpu_custom_call" | custom-call | tf_op jit(solution)/shard_map/pallas_call | solution.py:353

commit v3 on v2

--- a/solution.py
+++ b/solution.py
@@ -32,7 +32,7 @@
     emb, gw1, gw2, ew1, ew2, pw1, pw2, dw1,
     base, mall, dsum_w,
     emb_f, gw1_f, gw2_f, ew1_f, ew2_f, pw1_f, pw2_f, dw1_f,
-    lat, xs, own, psend, precv, half_send, half_recv, m1, bsend, srcs, wide,
+    xb, xs, own, psend, precv, half_send, half_recv, m1, bsend, srcs, wide,
     loc_sem, wsend_sem, wrecv_sem, as_sem, ar_sem, hs_sem, hr_sem, bs_sem, br_sem,
     gs_sem, gr_sem, fs_sem, fr_sem,
 ):
@@ -45,7 +45,6 @@
     prv = lax.rem(sec + S - 1, S)
     mrows = emb.shape[0]
     rows = mrows // M_BLK
-    g_blk = lat.shape[1]
     cols = pl.ds(pl.multiple_of(c * hw, hw), hw)
     ocols = pl.ds(pl.multiple_of(oc * hw, hw), hw)
 
@@ -72,6 +71,8 @@
         pl.semaphore_signal(
             barrier, inc=1, device_id={"band": lax.rem(me + d, B)}, device_id_type=MESH
         )
+    for g in range(x.shape[1] // rows):
+        xb[g] = x[:, g * rows : (g + 1) * rows]
     pl.semaphore_wait(barrier, B + 2)
 
     remote = [
@@ -87,27 +88,19 @@
         local[i].wait()
         remote[i].wait_recv()
 
+    def hidden(left):
+        pre = lax.dot_general(
+            left, gw1_f[...], (((0,), (0,)), ((), ())), preferred_element_type=F32
+        )
+        return norm_silu(pre, ggain[...])
+
+    chunk = 2 * rows
+    local[1].wait()
     arrived(0)
-    arrived(1)
-
-    chunk = 2 * rows
-
-    def grid_step(i, _):
-        r = pl.ds(pl.multiple_of(i * chunk, chunk), chunk)
-        pre = lax.dot_general(
-            x[:, r], gw1_f[...], (((0,), (0,)), ((), ())), preferred_element_type=F32
-        )
-        h = norm_silu(pre, ggain[...])
-        latent = mm(h, gw2_f[...]).astype(BF16)
-        for k in range(2):
-            for j in range(2):
-                lat[k, 2 * i + j] = latent[j * rows : (j + 1) * rows, k * hw : (k + 1) * hw]
-        return 0
-
-    lax.fori_loop(0, g_blk // 2, grid_step, 0, unroll=2)
-
-    for e in range(E):
-        xs[e * rows : (e + 1) * rows, :] = lat[c, esrc[e]]
+
+    for e in range(0, E, 2):
+        left = jnp.concatenate([xb[esrc[e]], xb[esrc[e + 1]]], axis=1)
+        xs[e * rows : (e + 2) * rows, :] = mm(hidden(left), gw2_f[:, cols]).astype(BF16)
 
     def part_for(q):
         lo = jnp.int32(0)
@@ -145,16 +138,16 @@
     arrived(2)
     arrived(3)
     wide[...] = mm(emb_f[...], ew1_f[0])
+    remote[1].wait_recv()
     arrived(4)
 
     def base_step(i, _):
-        left = jnp.concatenate([lat[0, 2 * i], lat[0, 2 * i + 1]], axis=0)
-        right = jnp.concatenate([lat[1, 2 * i], lat[1, 2 * i + 1]], axis=0)
-        out = mm(left, dw1_f[:hw, :]) + mm(right, dw1_f[hw:, :])
-        base[pl.ds(pl.multiple_of(i * chunk, chunk), chunk), :] = out.astype(BF16)
-        return 0
-
-    lax.fori_loop(0, g_blk // 2, base_step, 0)
+        r = pl.ds(pl.multiple_of(i * chunk, chunk), chunk)
+        latent = mm(hidden(x[:, r]), gw2_f[...]).astype(BF16)
+        base[r, :] = mm(latent, dw1_f[...]).astype(BF16)
+        return 0
+
+    lax.fori_loop(0, x.shape[1] // chunk, base_step, 0, unroll=2)
 
     def take_step(d, _):
         band_copy(d).wait_recv()
@@ -259,37 +252,38 @@
 
 def back_kernel(B, E, counts, esrc, etgt, base, mall, dsum_w, dblk, dgain, dw2, out, acc):
     rows = dblk.shape[1]
-    g_blk = acc.shape[0]
     hw = mall.shape[-1]
-    for g in range(g_blk):
-        acc[g] = base[g * rows : (g + 1) * rows, :].astype(F32)
-
-    def edge(e, _):
-        peer = jnp.int32(0)
-        end = jnp.int32(0)
-        for p in range(B):
-            end = end + counts[p]
-            peer = peer + jnp.where(end <= e, 1, 0)
-        r = pl.ds(pl.multiple_of(etgt[e] * rows, rows), rows)
-        add = jnp.zeros((rows, 2 * hw), F32)
-        for k in range(2):
-            msg = mm(dblk[e], mall[k, peer, r, :]).astype(BF16)
-            add = add + mm(msg, dsum_w[k * hw : (k + 1) * hw, :])
-        acc[esrc[e]] += add
-        return 0
-
-    lax.fori_loop(0, E, edge, 0, unroll=4)
-
-    def final(i, _):
-        v = jnp.concatenate([acc[2 * i], acc[2 * i + 1]], axis=0)
-        h = norm_silu(v, dgain[...])
-        r = pl.ds(pl.multiple_of(i * 2 * rows, 2 * rows), 2 * rows)
+    step = pl.program_id(0)
+    held = base.shape[0] // rows
+
+    @pl.when(step == 0)
+    def _():
+        acc[...] = jnp.zeros_like(acc)
+
+        def edge(e, _):
+            peer = jnp.int32(0)
+            end = jnp.int32(0)
+            for p in range(B):
+                end = end + counts[p]
+                peer = peer + jnp.where(end <= e, 1, 0)
+            r = pl.ds(pl.multiple_of(etgt[e] * rows, rows), rows)
+            add = jnp.zeros((rows, 2 * hw), F32)
+            for k in range(2):
+                msg = mm(dblk[e], mall[k, peer, r, :]).astype(BF16)
+                add = add + mm(msg, dsum_w[k * hw : (k + 1) * hw, :])
+            acc[esrc[e]] += add
+            return 0
+
+        lax.fori_loop(0, E, edge, 0, unroll=4)
+
+    for i in range(held // 2):
+        r = pl.ds(i * 2 * rows, 2 * rows)
+        g = step * held + 2 * i
+        v = base[r, :].astype(F32) + jnp.concatenate([acc[g], acc[g + 1]], axis=0)
         out[:, 0, r] = lax.dot_general(
-            dw2[...], h, (((1,), (1,)), ((), ())), preferred_element_type=F32
-        )
-        return 0
-
-    lax.fori_loop(0, g_blk // 2, final, 0, unroll=2)
+            dw2[...], norm_silu(v, dgain[...]), (((1,), (1,)), ((), ())),
+            preferred_element_type=F32,
+        )
 
 
 def local(
@@ -325,7 +319,7 @@
             pltpu.VMEM((2, lat_w, lat_w), BF16),
             pltpu.VMEM((lat_w, lat_w), BF16),
             pltpu.VMEM((lat_w, lat_w), BF16),
-            pltpu.VMEM((2, g_blk, rows, hw), BF16),
+            pltpu.VMEM((g_blk, ch, rows), BF16),
             pltpu.VMEM((E * rows, hw), BF16),
             pltpu.VMEM((mrows, hw), F32),
             pltpu.VMEM((B - 1, mrows, hw), BF16),
@@ -353,8 +347,9 @@
     out = pl.pallas_call(
         functools.partial(back_kernel, B, E),
         out_shape=jax.ShapeDtypeStruct((ch, 1, n), F32),
-        in_specs=[smem] * 3 + [vmem] * 6,
-        out_specs=vmem,
+        grid=(4,),
+        in_specs=[smem] * 3 + [pl.BlockSpec((n // 4, lat_w), lambda i: (i, 0))] + [vmem] * 5,
+        out_specs=pl.BlockSpec((ch, 1, n // 4), lambda i: (0, 0, i)),
         scratch_shapes=[pltpu.VMEM((g_blk, rows, lat_w), F32)],
         compiler_params=pltpu.CompilerParams(vmem_limit_bytes=63 * 2**20),
     )(

time: 58.6 us -> 54.5 us (0.930)
  Pallas kernels: 58.4 us -> 54.3 us
    pallas_call x1, Pallas kernels: 49.8 us -> 46.1 us  [local(): pl.pallas_call(functools.partial(front_kernel, B, S, E, PE), out_shape=(j...]
where the time goes in v3:
time: 54.5 us; the launch traced here: 54.3 us
  Pallas kernels  54.3 us (100%)
    pallas_call x1, Pallas kernels, local(): pl.pallas_call(functools.partial(front_kernel, B, S, E, PE), out_shape=(j...  46.1 us
    pallas_call x1, Pallas kernels, local(): pl.pallas_call(functools.partial(back_kernel, B, E), out_shape=jax.ShapeD...  8.19 us

profile of v3, /device:TPU:25, one launch (start us, length us, event | category | flops | bytes accessed | tf_op | source)
XLA Modules:
  0.0 54.3 jit_solution(412258167900437170)
XLA Ops:
  0.0 46.1 %shard_map.217 = (bf16[2048,512]{1,0:T(8,128)(2,1)}, bf16[2,4,256,256]{3,2,1,0:T(8,128)(2,1)}, bf16[512,512]{1,0:T(8,128)(2,1)}) custom-call(s32[4]{0:T(128)} %bitcast.33, s32[8]{0:T(128)} %bitcast.35, s32[8]{0:T(128)} %bitcast.37, s32[8]{0:T(128)} %bitcast.39, s32[8]{0:T(128)} %bitcast.40, s32[2]{0:T(128)} %bitcast.41, bf16[227,2048]{1,0:T(8,128)(2,1)} %bitcast.23, ...), custom_call_target="tpu_custom_call" | custom-call | tf_op jit(solution)/shard_map/pallas_call | solution.py:304
  46.1 8.2 %shard_map.218 = f32[227,1,2048]{2,1,0:T(1,128)} custom-call(s32[4]{0:T(128)} %bitcast.34, s32[8]{0:T(128)} %bitcast.36, s32[8]{0:T(128)} %bitcast.38, bf16[2048,512]{1,0:T(8,128)(2,1)} %get-tuple-element.8.base, bf16[2,4,256,256]{3,2,1,0:T(8,128)(2,1)} %get-tuple-element.9.mall, bf16[512,512]{1,0:T(8,128)(2,1)} %get-tuple-element.10.dsum_w, ...), custom_call_target="tpu_custom_call" | custom-call | tf_op jit(solution)/shard_map/pallas_call | solution.py:347

commit v4 on v3

--- a/solution.py
+++ b/solution.py
@@ -28,12 +28,13 @@
 def front_kernel(
     B, S, E, PE,
     counts, esrc, etgt, psrc, ptgt, bound,
-    x, eblk, pblk, ggain, egain, pgain,
-    emb, gw1, gw2, ew1, ew2, pw1, pw2, dw1,
-    base, mall, dsum_w,
+    ggain, egain, pgain,
+    x_in, eblk_in, pblk_in, emb, gw1, gw2, ew1, ew2, pw1, pw2, dw1,
+    base_out, mall,
+    x, eblk, pblk, base, dsum_w,
     emb_f, gw1_f, gw2_f, ew1_f, ew2_f, pw1_f, pw2_f, dw1_f,
     xb, xs, own, psend, precv, half_send, half_recv, m1, bsend, srcs, wide,
-    loc_sem, wsend_sem, wrecv_sem, as_sem, ar_sem, hs_sem, hr_sem, bs_sem, br_sem,
+    in_sem, loc_sem, wsend_sem, wrecv_sem, as_sem, ar_sem, hs_sem, hr_sem, bs_sem, br_sem,
     gs_sem, gr_sem, fs_sem, fr_sem,
 ):
     me = lax.axis_index("band")
@@ -60,7 +61,11 @@
         (dw1.at[1], dsum_w.at[:, cols]),
     ]
     local = [pltpu.make_async_copy(s, d, loc_sem.at[i]) for i, (s, d) in enumerate(parts)]
-    for cp in local:
+    operands = [
+        pltpu.make_async_copy(s, d, in_sem.at[i])
+        for i, (s, d) in enumerate([(x_in, x), (eblk_in, eblk), (pblk_in, pblk)])
+    ]
+    for cp in operands[:1] + local + operands[1:]:
         cp.start()
 
     barrier = pltpu.get_barrier_semaphore()
@@ -71,6 +76,7 @@
         pl.semaphore_signal(
             barrier, inc=1, device_id={"band": lax.rem(me + d, B)}, device_id_type=MESH
         )
+    operands[0].wait()
     for g in range(x.shape[1] // rows):
         xb[g] = x[:, g * rows : (g + 1) * rows]
     pl.semaphore_wait(barrier, B + 2)
@@ -101,6 +107,8 @@
     for e in range(0, E, 2):
         left = jnp.concatenate([xb[esrc[e]], xb[esrc[e + 1]]], axis=1)
         xs[e * rows : (e + 2) * rows, :] = mm(hidden(left), gw2_f[:, cols]).astype(BF16)
+
+    operands[1].wait()
 
     def part_for(q):
         lo = jnp.int32(0)
@@ -149,6 +157,9 @@
 
     lax.fori_loop(0, x.shape[1] // chunk, base_step, 0, unroll=2)
 
+    save = pltpu.make_async_copy(base, base_out, in_sem.at[3])
+    save.start()
+
     def take_step(d, _):
         band_copy(d).wait_recv()
         own[...] += precv[d - 1].astype(F32)
@@ -192,6 +203,7 @@
     wide[...] = mm(one, pw1_f[0])
     to_next.wait_recv()
     to_prev.wait_recv()
+    operands[2].wait()
     ys = jnp.concatenate([srcs[psrc[e]] for e in range(PE)], axis=0)
     for m in range(M_BLK):
         pieces = []
@@ -201,8 +213,10 @@
         own[m * rows : (m + 1) * rows, :] = mm(jnp.concatenate(pieces, axis=1), ys)
     arrived(7)
     two = (one.astype(F32) + update(1, own[...], pw1_f, pgain, pw2_f)).astype(BF16)
+    arrived(8)
+    image = mm(two, dsum_w[...]).astype(BF16)
     for k in range(2):
-        mall[k, me] = two[:, k * hw : (k + 1) * hw]
+        mall[k, me] = image[:, k * hw : (k + 1) * hw]
 
     def out_copy(d):
         return pltpu.make_async_remote_copy(
@@ -241,7 +255,7 @@
         return 0
 
     lax.fori_loop(1, B, gather_start, 0, unroll=B <= 4)
-    arrived(8)
+    save.wait()
     to_next.wait_send()
     to_prev.wait_send()
     for cp in remote:
@@ -250,7 +264,7 @@
     lax.fori_loop(1, B, gather_end, 0, unroll=B <= 4)
 
 
-def back_kernel(B, E, counts, esrc, etgt, base, mall, dsum_w, dblk, dgain, dw2, out, acc):
+def back_kernel(B, E, counts, esrc, etgt, base, mall, dblk, dgain, dw2, out, acc):
     rows = dblk.shape[1]
     hw = mall.shape[-1]
     step = pl.program_id(0)
@@ -267,10 +281,7 @@
                 end = end + counts[p]
                 peer = peer + jnp.where(end <= e, 1, 0)
             r = pl.ds(pl.multiple_of(etgt[e] * rows, rows), rows)
-            add = jnp.zeros((rows, 2 * hw), F32)
-            for k in range(2):
-                msg = mm(dblk[e], mall[k, peer, r, :]).astype(BF16)
-                add = add + mm(msg, dsum_w[k * hw : (k + 1) * hw, :])
+            add = jnp.concatenate([mm(dblk[e], mall[k, peer, r, :]) for k in range(2)], axis=1)
             acc[esrc[e]] += add
             return 0
 
@@ -301,16 +312,20 @@
     vmem = pl.BlockSpec(memory_space=pltpu.VMEM)
     hbm = pl.BlockSpec(memory_space=pl.ANY)
     dma = pltpu.SemaphoreType.DMA
-    base, mall, dsum_w = pl.pallas_call(
+    base, mall = pl.pallas_call(
         functools.partial(front_kernel, B, S, E, PE),
         out_shape=(
             jax.ShapeDtypeStruct((n, lat_w), BF16),
             jax.ShapeDtypeStruct((2, B, mrows, hw), BF16),
-            jax.ShapeDtypeStruct((lat_w, lat_w), BF16),
         ),
-        in_specs=[smem] * 6 + [vmem] * 6 + [hbm] * 8,
-        out_specs=(vmem, vmem, vmem),
+        in_specs=[smem] * 6 + [vmem] * 3 + [hbm] * 11,
+        out_specs=(hbm, vmem),
         scratch_shapes=[
+            pltpu.VMEM((ch, n), BF16),
+            pltpu.VMEM((E, rows, rows), BF16),
+            pltpu.VMEM((PE, rows, rows), BF16),
+            pltpu.VMEM((n, lat_w), BF16),
+            pltpu.VMEM((lat_w, lat_w), BF16),
             pltpu.VMEM((mrows, lat_w), BF16),
             pltpu.VMEM((ch, lat_w), BF16),
             pltpu.VMEM((lat_w, lat_w), BF16),
@@ -330,7 +345,7 @@
             pltpu.VMEM((2, rows, hw), BF16),
             pltpu.VMEM((M_BLK + 2, rows, hw), BF16),
             pltpu.VMEM((mrows, lat_w), F32),
-            dma((9,)), dma((9,)), dma((9,)),
+            dma((4,)), dma((9,)), dma((9,)), dma((9,)),
             dma((B - 1,)), dma((B - 1,)),
             dma((2,)), dma((2,)), dma((2,)), dma((2,)),
             dma((B - 1,)), dma((B - 1,)), dma((B - 1,)), dma((B - 1,)),
@@ -340,21 +355,20 @@
         ),
     )(
         counts[0, 0], esrc[0, 0], etgt[0, 0], psrc[0, 0], ptgt[0, 0], bound.reshape(-1),
-        grid_inputs[0, 0].T, eblk[0, 0], pblk[0, 0],
         ggain.reshape(1, -1), egain.reshape(1, -1), pgain.reshape(1, -1),
-        emb[0, 0], gw1, gw2, ew1, ew2, pw1, pw2, dw1,
+        grid_inputs[0, 0].T, eblk[0, 0], pblk[0, 0], emb[0, 0], gw1, gw2, ew1, ew2, pw1, pw2, dw1,
     )
     out = pl.pallas_call(
         functools.partial(back_kernel, B, E),
         out_shape=jax.ShapeDtypeStruct((ch, 1, n), F32),
         grid=(4,),
-        in_specs=[smem] * 3 + [pl.BlockSpec((n // 4, lat_w), lambda i: (i, 0))] + [vmem] * 5,
+        in_specs=[smem] * 3 + [pl.BlockSpec((n // 4, lat_w), lambda i: (i, 0))] + [vmem] * 4,
         out_specs=pl.BlockSpec((ch, 1, n // 4), lambda i: (0, 0, i)),
         scratch_shapes=[pltpu.VMEM((g_blk, rows, lat_w), F32)],
         compiler_params=pltpu.CompilerParams(vmem_limit_bytes=63 * 2**20),
     )(
         counts[0, 0], esrc[0, 0], etgt[0, 0],
-        base, mall, dsum_w, dblk[0, 0], dgain.reshape(1, -1), dw2.T,
+        base, mall, dblk[0, 0], dgain.reshape(1, -1), dw2.T,
     )
     return jnp.transpose(out, (1, 2, 0))[None]
 

time: 54.5 us -> 52 us (0.954)
  Pallas kernels: 54.3 us -> 51.8 us
    pallas_call x1, Pallas kernels: 8.19 us -> 6.69 us  [local(): pl.pallas_call(functools.partial(back_kernel, B, E), out_shape=jax.ShapeD...]
    pallas_call x1, Pallas kernels: 46.1 us -> 45.1 us  [local(): pl.pallas_call(functools.partial(front_kernel, B, S, E, PE), out_shape=(j...]
where the time goes in v4:
time: 52 us; the launch traced here: 51.8 us
  Pallas kernels  51.8 us (100%)
    pallas_call x1, Pallas kernels, local(): pl.pallas_call(functools.partial(front_kernel, B, S, E, PE), out_shape=(j...  45.1 us
    pallas_call x1, Pallas kernels, local(): pl.pallas_call(functools.partial(back_kernel, B, E), out_shape=jax.ShapeD...  6.69 us

profile of v4, /device:TPU:25, one launch (start us, length us, event | category | flops | bytes accessed | tf_op | source)
XLA Modules:
  0.0 51.8 jit_solution(3115061726736513326)
XLA Ops:
  0.0 45.1 %shard_map.217 = (bf16[2048,512]{1,0:T(8,128)(2,1)}, bf16[2,4,256,256]{3,2,1,0:T(8,128)(2,1)}) custom-call(s32[4]{0:T(128)} %bitcast.33, s32[8]{0:T(128)} %bitcast.35, s32[8]{0:T(128)} %bitcast.37, s32[8]{0:T(128)} %bitcast.39, s32[8]{0:T(128)} %bitcast.40, s32[2]{0:T(128)} %bitcast.41, f32[1,512]{1,0:T(1,128)} %bitcast.29, f32[1,512]{1,0:T(1,128)} %bitcast.30, ...), custom_call_target="tpu_custom_call" | custom-call | tf_op jit(solution)/shard_map/pallas_call | solution.py:315
  45.1 6.7 %shard_map.218 = f32[227,1,2048]{2,1,0:T(1,128)} custom-call(s32[4]{0:T(128)} %bitcast.34, s32[8]{0:T(128)} %bitcast.36, s32[8]{0:T(128)} %bitcast.38, bf16[2048,512]{1,0:T(8,128)(2,1)} %get-tuple-element.7.base, bf16[2,4,256,256]{3,2,1,0:T(8,128)(2,1)} %get-tuple-element.8.mall, bf16[8,128,128]{2,1,0:T(8,128)(2,1)} %bitcast.24, f32[1,512]{1,0:T(1,128)} %bitcast.32, ...), custom_call_target="tpu_custom_call" | custom-call | tf_op jit(solution)/shard_map/pallas_call | solution.py:361

commit v5 on v4

--- a/solution.py
+++ b/solution.py
@@ -21,8 +21,8 @@
     n = 1.0 / v.shape[-1]
     center = v - jnp.sum(v, axis=-1, keepdims=True) * n
     spread = jnp.sum(center * center, axis=-1, keepdims=True) * n
-    half = center * lax.rsqrt(spread + 1e-5) * (0.5 * gain)
-    return (half + half * jnp.tanh(half)).astype(BF16)
+    half = (center * lax.rsqrt(spread + 1e-5) * (0.5 * gain)).astype(BF16)
+    return half + half * jnp.tanh(half)
 
 
 def front_kernel(

time: 52 us -> 51.9 us (level)
  no operation moved by 1% of the time
where the time goes in v5:
time: 51.9 us; the launch traced here: 51.7 us
  Pallas kernels  51.7 us (100%)
    pallas_call x1, Pallas kernels, local(): pl.pallas_call(functools.partial(front_kernel, B, S, E, PE), out_shape=(j...  45.1 us
    pallas_call x1, Pallas kernels, local(): pl.pallas_call(functools.partial(back_kernel, B, E), out_shape=jax.ShapeD...  6.59 us

profile of v5, /device:TPU:25, one launch (start us, length us, event | category | flops | bytes accessed | tf_op | source)
XLA Modules:
  0.0 51.7 jit_solution(9059485708632978645)
XLA Ops:
  0.0 45.1 %shard_map.217 = (bf16[2048,512]{1,0:T(8,128)(2,1)}, bf16[2,4,256,256]{3,2,1,0:T(8,128)(2,1)}) custom-call(s32[4]{0:T(128)} %bitcast.33, s32[8]{0:T(128)} %bitcast.35, s32[8]{0:T(128)} %bitcast.37, s32[8]{0:T(128)} %bitcast.39, s32[8]{0:T(128)} %bitcast.40, s32[2]{0:T(128)} %bitcast.41, f32[1,512]{1,0:T(1,128)} %bitcast.29, f32[1,512]{1,0:T(1,128)} %bitcast.30, ...), custom_call_target="tpu_custom_call" | custom-call | tf_op jit(solution)/shard_map/pallas_call | solution.py:315
  45.1 6.6 %shard_map.218 = f32[227,1,2048]{2,1,0:T(1,128)} custom-call(s32[4]{0:T(128)} %bitcast.34, s32[8]{0:T(128)} %bitcast.36, s32[8]{0:T(128)} %bitcast.38, bf16[2048,512]{1,0:T(8,128)(2,1)} %get-tuple-element.7.base, bf16[2,4,256,256]{3,2,1,0:T(8,128)(2,1)} %get-tuple-element.8.mall, bf16[8,128,128]{2,1,0:T(8,128)(2,1)} %bitcast.24, f32[1,512]{1,0:T(1,128)} %bitcast.32, ...), custom_call_target="tpu_custom_call" | custom-call | tf_op jit(solution)/shard_map/pallas_call | solution.py:361
